TPU v7x, 128 devices: a whole 4x4x4 slice. The times are simulated.
128 devices in a mesh: shard: 4 (over z), context: 8 (over x, core), tensor: 4 (over y).
Axes of the slice: x: 4, y: 4, z: 4, core: 2. Of those that a mesh axis runs over, the one named last changes fastest.
Arguments:
- tokens_in: bfloat16 [8192, 2048], P(('shard', 'context')), may hold values from -6 to 6
- cotangent: bfloat16 [8192, 2048], P(('shard', 'context')), may hold values from -6 to 6
- segments: int32 [4, 2048], P('shard'), may hold values from 0 to 4, as said below
- positions: int32 [8192], P(('shard', 'context')), may hold values from 0 to 2047, as said below
- norm1_gain: bfloat16 [2048], P(('shard', 'context')), may hold values from 0.099609375 to 1.8984375
- q_weight: bfloat16 [2048, 2048], P(('shard', 'context'), 'tensor'), may hold values from -0.125 to 0.125
- k_weight: bfloat16 [2048, 2048], P(('shard', 'context'), 'tensor'), may hold values from -0.125 to 0.125
- v_weight: bfloat16 [2048, 2048], P(('shard', 'context'), 'tensor'), may hold values from -0.125 to 0.125
- o_weight: bfloat16 [2048, 2048], P('tensor', ('shard', 'context')), may hold values from -4 to 4
- norm2_gain: bfloat16 [2048], P(('shard', 'context')), may hold values from 0.099609375 to 1.8984375
- gate_weight: bfloat16 [2048, 8192], P(('shard', 'context'), 'tensor'), may hold values from -0.125 to 0.125
- up_weight: bfloat16 [2048, 8192], P(('shard', 'context'), 'tensor'), may hold values from -0.125 to 0.125
- down_weight: bfloat16 [8192, 2048], P('tensor', ('shard', 'context')), may hold values from -0.0625 to 0.0625
Outputs:
- layer_out: bfloat16 [8192, 2048], P(('shard', 'context'))
- input_grad: bfloat16 [8192, 2048], P(('shard', 'context'))
- grad_norm1: float32 [2048], P(('shard', 'context'))
- grad_q: float32 [2048, 2048], P(('shard', 'context'), 'tensor')
- grad_k: float32 [2048, 2048], P(('shard', 'context'), 'tensor')
- grad_v: float32 [2048, 2048], P(('shard', 'context'), 'tensor')
- grad_o: float32 [2048, 2048], P('tensor', ('shard', 'context'))
- grad_norm2: float32 [2048], P(('shard', 'context'))
- grad_gate: float32 [2048, 8192], P(('shard', 'context'), 'tensor')
- grad_up: float32 [2048, 8192], P(('shard', 'context'), 'tensor')
- grad_down: float32 [8192, 2048], P('tensor', ('shard', 'context'))
Inputs may be any that keep to these rules, and one draw needn't show every extreme that they name: `segments`: within a sequence the document numbers never fall and rise by one at each boundary; every sequence holds documents 0 to 4. Within one document the positions rise by one from token to token.
All inputs are finite; a program needn't handle non-finite values.
Results may differ from a plain program's by a relative error of at most 0.03.
Values may be sent and summed in bfloat16 or wider, within the bound.
A program may use at most 192 MiB of HBM per device.

v0:
```python
import math

import jax
import jax.numpy as jnp
from jax import lax
from jax.sharding import PartitionSpec as P

HEAD_DIM = 64


epsilon = 1e-05
rope_base = 130000.0
masked_low = -1000000000.0


def gather_turned(arrays, axis, dims):
    turned = [jnp.moveaxis(a, dim, 0) for a, dim in zip(arrays, dims)]
    widths = [t[0].size for t in turned]
    both = jnp.concatenate([t.reshape(-1, w) for t, w in zip(turned, widths)], axis=1)
    whole = lax.all_gather(both, axis, axis=0, tiled=True)
    pieces = jnp.split(whole, [sum(widths[:k]) for k in range(1, len(widths))], axis=1)
    return tuple(
        (
            jnp.moveaxis(b.reshape(-1, *t.shape[1:]), 0, dim)
            for b, t, dim in zip(pieces, turned, dims)
        )
    )


def sent_together(arrays, axis, dim, along):
    ends, at = ([], 0)
    for a in arrays[:-1]:
        at += a.shape[along]
        ends.append(at)
    both = jnp.concatenate(arrays, axis=along)
    return tuple(jnp.split(lax.all_gather(both, axis, axis=dim, tiled=True), ends, axis=along))


def in_one_piece(arrays, axis, dim, along):
    columns = [a.reshape(*a.shape[:along], -1) for a in arrays]
    both = jnp.concatenate(columns, axis=along)
    whole, at, done = (lax.psum_scatter(both, axis, scatter_dimension=dim, tiled=True), 0, [])
    for a, column in zip(arrays, columns):
        piece = whole[..., at : at + column.shape[along]]
        done.append(piece.reshape(*piece.shape[:along], *a.shape[along:]))
        at += column.shape[along]
    return tuple(done)


def in_one_piece_2(arrays, axis, dim, along):
    ends, at = ([], 0)
    for a in arrays[:-1]:
        at += a.shape[along]
        ends.append(at)
    both = jnp.concatenate(arrays, axis=along)
    return tuple(
        jnp.split(lax.psum_scatter(both, axis, scatter_dimension=dim, tiled=True), ends, axis=along)
    )


def angle_tables(positions):
    half = HEAD_DIM // 2
    frequency = rope_base ** (-(jnp.arange(half, dtype=jnp.float32) * 2.0) / HEAD_DIM)
    angle = positions.astype(jnp.float32)[:, None] * frequency[None, :]
    return (jnp.cos(angle)[:, None, :], jnp.sin(angle)[:, None, :])


def rotate(vectors, cosine, sine):
    half = HEAD_DIM // 2
    first = vectors[..., :half]
    second = vectors[..., half:]
    return jnp.concatenate(
        [first * cosine - second * sine, second * cosine + first * sine], axis=-1
    )


def block_scores(queries, q_seg, q_index, key_block, k_seg, k_index):
    allowed = ((q_seg[:, None] == k_seg[None, :]) & (k_index[None, :] <= q_index[:, None]))[None]
    raw_scores = jnp.einsum("qhd,khd->hqk", queries, key_block, preferred_element_type=jnp.float32)
    return (allowed, jnp.where(allowed, raw_scores * HEAD_DIM ** (-0.5), masked_low))


def forward_block(state, queries, q_seg, q_index, key_block, value_block, k_seg, k_index):
    summed, peak, total = state
    allowed, scores = block_scores(queries, q_seg, q_index, key_block, k_seg, k_index)
    new_peak = jnp.maximum(peak, jnp.max(scores, axis=-1))
    weights = jnp.where(allowed, jnp.exp(scores - new_peak[..., None]), 0.0)
    factor = jnp.exp(peak - new_peak)
    total = total * factor + jnp.sum(weights, axis=-1)
    update = jnp.einsum(
        "hqk,khd->qhd",
        weights.astype(jnp.bfloat16),
        value_block,
        preferred_element_type=jnp.float32,
    )
    summed = summed * jnp.transpose(factor)[:, :, None] + update
    return (summed, new_peak, total)


def backward_block(
    queries, q_seg, q_index, peak, d_sum, center, key_block, value_block, k_seg, k_index
):
    allowed, scores = block_scores(queries, q_seg, q_index, key_block, k_seg, k_index)
    weights = jnp.where(allowed, jnp.exp(scores - peak[..., None]), 0.0)
    d_prob = jnp.einsum("qhd,khd->hqk", d_sum, value_block, preferred_element_type=jnp.float32)
    d_raw = (weights * (d_prob - center[..., None]) * HEAD_DIM ** (-0.5)).astype(jnp.bfloat16)
    d_query = jnp.einsum("hqk,khd->qhd", d_raw, key_block, preferred_element_type=jnp.float32)
    d_key = jnp.einsum("hqk,qhd->khd", d_raw, queries, preferred_element_type=jnp.float32)
    d_value = jnp.einsum(
        "hqk,qhd->khd", weights.astype(jnp.bfloat16), d_sum, preferred_element_type=jnp.float32
    )
    return (d_query, d_key, d_value)


def norm_back(d_normed, unit, scale, gain):
    grad_gain = jnp.sum(d_normed * unit, axis=0)
    scaled = d_normed * gain
    return (grad_gain, scale * (scaled - unit * jnp.mean(scaled * unit, axis=-1, keepdims=True)))


def body(
    tokens_in,
    cotangent,
    segments,
    positions,
    norm1_gain,
    q_weight,
    k_weight,
    v_weight,
    o_weight,
    norm2_gain,
    gate_weight,
    up_weight,
    down_weight,
):
    rows = tokens_in.shape[0]
    heads_local = q_weight.shape[1] // HEAD_DIM
    gain_one, q_full, k_full, v_full, o_full = gather_turned(
        (norm1_gain, q_weight, k_weight, v_weight, o_weight), ("shard", "context"), (0, 0, 0, 0, 1)
    )
    gain_two, gate_full, up_full, down_full = gather_turned(
        (norm2_gain, gate_weight, up_weight, down_weight), ("shard", "context"), (0, 0, 0, 1)
    )
    gain_one = gain_one.astype(jnp.float32)
    gain_two = gain_two.astype(jnp.float32)
    context_index = lax.axis_index("context")
    seq_segs = segments[0]
    q_start = context_index * rows
    local_index = jnp.arange(rows, dtype=jnp.int32)
    q_index = q_start + local_index
    q_seg = lax.dynamic_slice_in_dim(seq_segs, q_start, rows)
    inputs = tokens_in.astype(jnp.float32)
    scale_one = lax.rsqrt(jnp.mean(inputs * inputs, axis=-1, keepdims=True) + epsilon)
    unit_one = inputs * scale_one
    normed_one = (unit_one * gain_one).astype(jnp.bfloat16)
    q_lin = jnp.dot(normed_one, q_full, preferred_element_type=jnp.float32).reshape(
        rows, heads_local, HEAD_DIM
    )
    k_lin = jnp.dot(normed_one, k_full, preferred_element_type=jnp.float32).reshape(
        rows, heads_local, HEAD_DIM
    )
    v_lin = jnp.dot(normed_one, v_full, preferred_element_type=jnp.float32).reshape(
        rows, heads_local, HEAD_DIM
    )
    cosine, sine = angle_tables(positions)
    queries = rotate(q_lin, cosine, sine).astype(jnp.bfloat16)
    keys = rotate(k_lin, cosine, sine).astype(jnp.bfloat16)
    values = v_lin.astype(jnp.bfloat16)
    initial = (
        jnp.zeros((rows, heads_local, HEAD_DIM), jnp.float32),
        jnp.full((heads_local, rows), masked_low, jnp.float32),
        jnp.zeros((heads_local, rows), jnp.float32),
    )
    key_all, value_all = sent_together((keys, values), "context", 0, 1)
    seq_len = key_all.shape[0]
    block = math.gcd(seq_len, 512)
    count = seq_len // block
    key_blocks = key_all.reshape(count, block, heads_local, HEAD_DIM)
    value_blocks = value_all.reshape(count, block, heads_local, HEAD_DIM)
    seg_blocks = seq_segs.reshape(count, block)
    index_blocks = jnp.arange(seq_len, dtype=jnp.int32).reshape(count, block)

    def fold_step(state, pieces):
        key_block, value_block, k_seg, k_index = pieces
        return (
            forward_block(state, queries, q_seg, q_index, key_block, value_block, k_seg, k_index),
            None,
        )

    state, unused = lax.scan(
        fold_step, initial, (key_blocks, value_blocks, seg_blocks, index_blocks)
    )
    summed, peak, total = state
    total_qh = jnp.transpose(total)[:, :, None]
    attended = summed / total_qh
    attended_low = attended.astype(jnp.bfloat16).reshape(rows, heads_local * HEAD_DIM)
    branch = lax.psum(
        jnp.dot(attended_low, o_full, preferred_element_type=jnp.float32).astype(jnp.bfloat16),
        "tensor",
    ).astype(jnp.float32)
    middle = inputs + branch
    scale_two = lax.rsqrt(jnp.mean(middle * middle, axis=-1, keepdims=True) + epsilon)
    unit_two = middle * scale_two
    normed_two = (unit_two * gain_two).astype(jnp.bfloat16)
    gate = jnp.dot(normed_two, gate_full, preferred_element_type=jnp.float32)
    upper = jnp.dot(normed_two, up_full, preferred_element_type=jnp.float32)
    sigmoid = jax.nn.sigmoid(gate)
    silu = gate * sigmoid
    hidden = (silu * upper).astype(jnp.bfloat16)
    mixed = lax.psum(
        jnp.dot(hidden, down_full, preferred_element_type=jnp.float32).astype(jnp.bfloat16),
        "tensor",
    ).astype(jnp.float32)
    layer_out = (middle + mixed).astype(jnp.bfloat16)
    grad_down_term = jnp.einsum("tf,td->fd", hidden, cotangent, preferred_element_type=jnp.float32)
    d_hidden = jnp.einsum("td,fd->tf", cotangent, down_full, preferred_element_type=jnp.float32)
    d_gate = (d_hidden * upper * (sigmoid * (1.0 + gate * (1.0 - sigmoid)))).astype(jnp.bfloat16)
    d_upper = (d_hidden * silu).astype(jnp.bfloat16)
    grad_gate_term = jnp.einsum("td,tf->df", normed_two, d_gate, preferred_element_type=jnp.float32)
    grad_up_term = jnp.einsum("td,tf->df", normed_two, d_upper, preferred_element_type=jnp.float32)
    d_normed_two = lax.psum(
        (
            jnp.einsum("tf,df->td", d_gate, gate_full, preferred_element_type=jnp.float32)
            + jnp.einsum("tf,df->td", d_upper, up_full, preferred_element_type=jnp.float32)
        ).astype(jnp.bfloat16),
        "tensor",
    ).astype(jnp.float32)
    gain_two_term, d_middle_norm = norm_back(d_normed_two, unit_two, scale_two, gain_two)
    grad_norm2, grad_gate, grad_up, grad_down = (
        *tuple(
            (
                part.astype(jnp.float32)
                for part in in_one_piece(
                    (
                        gain_two_term.astype(jnp.bfloat16),
                        grad_gate_term.astype(jnp.bfloat16),
                        grad_up_term.astype(jnp.bfloat16),
                    ),
                    ("shard", "context"),
                    0,
                    1,
                )
            )
        ),
        lax.psum_scatter(
            grad_down_term.astype(jnp.bfloat16),
            ("shard", "context"),
            scatter_dimension=1,
            tiled=True,
        ).astype(jnp.float32),
    )
    d_middle = cotangent.astype(jnp.float32) + d_middle_norm
    d_branch = d_middle.astype(jnp.bfloat16)
    grad_o_term = jnp.einsum(
        "tq,td->qd", attended_low, d_branch, preferred_element_type=jnp.float32
    )
    d_attended = jnp.einsum(
        "td,qd->tq", d_branch, o_full, preferred_element_type=jnp.float32
    ).reshape(rows, heads_local, HEAD_DIM)
    d_sum = (d_attended / total_qh).astype(jnp.bfloat16)
    center = jnp.transpose(jnp.sum(d_attended * attended, axis=-1)) / total

    def back_step(d_query, pieces):
        key_block, value_block, k_seg, k_index = pieces
        part_query, part_key, part_value = backward_block(
            queries, q_seg, q_index, peak, d_sum, center, key_block, value_block, k_seg, k_index
        )
        return (d_query + part_query, (part_key, part_value))

    d_queries, (key_terms, value_terms) = lax.scan(
        back_step,
        jnp.zeros((rows, heads_local, HEAD_DIM), jnp.float32),
        (key_blocks, value_blocks, seg_blocks, index_blocks),
    )
    d_keys, d_values = tuple(
        (
            part.astype(jnp.float32)
            for part in in_one_piece_2(
                (
                    key_terms.reshape(seq_len, heads_local, HEAD_DIM).astype(jnp.bfloat16),
                    value_terms.reshape(seq_len, heads_local, HEAD_DIM).astype(jnp.bfloat16),
                ),
                "context",
                0,
                1,
            )
        )
    )
    d_q_lin = (
        rotate(d_queries, cosine, -sine).astype(jnp.bfloat16).reshape(rows, heads_local * HEAD_DIM)
    )
    d_k_lin = (
        rotate(d_keys, cosine, -sine).astype(jnp.bfloat16).reshape(rows, heads_local * HEAD_DIM)
    )
    d_v_lin = d_values.astype(jnp.bfloat16).reshape(rows, heads_local * HEAD_DIM)
    grad_q_term = jnp.einsum("td,tq->dq", normed_one, d_q_lin, preferred_element_type=jnp.float32)
    grad_k_term = jnp.einsum("td,tq->dq", normed_one, d_k_lin, preferred_element_type=jnp.float32)
    grad_v_term = jnp.einsum("td,tq->dq", normed_one, d_v_lin, preferred_element_type=jnp.float32)
    d_normed_one = jnp.einsum("tq,dq->td", d_q_lin, q_full, preferred_element_type=jnp.float32)
    d_normed_one = d_normed_one + jnp.einsum(
        "tq,dq->td", d_k_lin, k_full, preferred_element_type=jnp.float32
    )
    d_normed_one = d_normed_one + jnp.einsum(
        "tq,dq->td", d_v_lin, v_full, preferred_element_type=jnp.float32
    )
    d_normed_one = lax.psum(d_normed_one.astype(jnp.bfloat16), "tensor").astype(jnp.float32)
    gain_one_term, d_input_norm = norm_back(d_normed_one, unit_one, scale_one, gain_one)
    grad_norm1, grad_q, grad_k, grad_v, grad_o = (
        *tuple(
            (
                part.astype(jnp.float32)
                for part in in_one_piece(
                    (
                        gain_one_term.astype(jnp.bfloat16),
                        grad_q_term.astype(jnp.bfloat16),
                        grad_k_term.astype(jnp.bfloat16),
                        grad_v_term.astype(jnp.bfloat16),
                    ),
                    ("shard", "context"),
                    0,
                    1,
                )
            )
        ),
        lax.psum_scatter(
            grad_o_term.astype(jnp.bfloat16), ("shard", "context"), scatter_dimension=1, tiled=True
        ).astype(jnp.float32),
    )
    input_grad = (d_middle + d_input_norm).astype(jnp.bfloat16)
    return (
        layer_out,
        input_grad,
        grad_norm1,
        grad_q,
        grad_k,
        grad_v,
        grad_o,
        grad_norm2,
        grad_gate,
        grad_up,
        grad_down,
    )


def solution(mesh):
    placed = (
        P(("shard", "context"), None),
        P(("shard", "context"), None),
        P("shard", None),
        P(("shard", "context")),
        P(("shard", "context")),
        P(("shard", "context"), "tensor"),
        P(("shard", "context"), "tensor"),
        P(("shard", "context"), "tensor"),
        P("tensor", ("shard", "context")),
        P(("shard", "context")),
        P(("shard", "context"), "tensor"),
        P(("shard", "context"), "tensor"),
        P("tensor", ("shard", "context")),
    )
    return jax.shard_map(
        body,
        mesh=mesh,
        in_specs=placed,
        out_specs=(
            P(("shard", "context"), None),
            P(("shard", "context"), None),
            P(("shard", "context")),
            P(("shard", "context"), "tensor"),
            P(("shard", "context"), "tensor"),
            P(("shard", "context"), "tensor"),
            P("tensor", ("shard", "context")),
            P(("shard", "context")),
            P(("shard", "context"), "tensor"),
            P(("shard", "context"), "tensor"),
            P("tensor", ("shard", "context")),
        ),
        check_vma=False,
    )
```

profile of v0, /device:TPU:0, one launch (start us, length us, event | category | flops | bytes accessed | tf_op | source)
XLA Modules:
  0.0 950.8 jit_solution(14489769694922659402)
XLA Ops:
  12.4 55.2 %all-gather.4.cloned.1.call-done = bf16[2048,2049]{1,0:T(8,128)(2,1)} async-done(((bf16[64,2049]{1,0:T(8,128)(2,1)}), bf16[2048,2049]{1,0:T(8,128)(2,1)}) %all-gather.4.cloned.1.call-update) | async-done | bytes 8392720 | tf_op jit(solution)/shard_map/all_gather | solution.py:20
  69.0 2.9 fusion.116
  72.0 3.7 fusion.108
  75.7 3.7 fusion.114
  81.8 34.3 %all-gather.6.cloned.1.call-done = bf16[2048,16,64]{0,2,1:T(8,128)(2,1)} async-done(((bf16[256,16,64]{0,2,1:T(8,128)(2,1)}), bf16[2048,16,64]{0,2,1:T(8,128)(2,1)}) %all-gather.6.cloned.1.call-update) | async-done | bytes 4194320 | tf_op jit(solution)/shard_map/all_gather | solution.py:36
  116.1 2.7 fusion.131
  120.7 21.0 %while.30 = (s32[]{:T(128)}, f32[256,8,64]{0,2,1:T(8,128)}, f32[8,256]{1,0:T(8,128)S(1)}, f32[8,256]{1,0:T(8,128)S(1)}, s32[256]{0:T(256)S(1)}, /*index=5*/s32[4...) while((s32[]{:T(128)}, f32[256,8,64]{0,2,1:T(8,128)}, ...), condition=%wide.region_4.5_spmd.clone, body=%wide.region_1.4_spmd.clone.sunk | while | flops 282865920 | bytes 19807448 | solution.py:190
  122.9 2.3 fusion.190
  128.1 2.3 fusion.190
  133.4 2.3 fusion.190
  138.6 2.3 fusion.190
  143.5 4.1 convolution_convert_fusion.7
  147.8 2.4 concatenate.38
  150.6 44.0 %all-reduce.5.cloned.1.call-done = bf16[256,2048]{1,0:T(8,128)(2,1)} async-done(((bf16[256,2048]{1,0:T(8,128)(2,1)}), bf16[256,2048]{1,0:T(8,128)(2,1)}) %all-reduce.5.cloned.1.call-update) | async-done | bytes 1048592 | tf_op jit(solution)/shard_map/psum | solution.py:197
  196.2 95.6 %all-gather.8.cloned.1.call-done = bf16[2048,6145]{1,0:T(8,128)(2,1)} async-done(((bf16[64,6145]{1,0:T(8,128)(2,1)}), bf16[2048,6145]{1,0:T(8,128)(2,1)}) %all-gather.8.cloned.1.call-update) | async-done | bytes 25169936 | tf_op jit(solution)/shard_map/all_gather | solution.py:20
  294.8 7.0 fusion.68
  301.9 6.6 fusion.74
  308.5 8.6 multiply_convert_fusion.2
  317.1 17.0 %fusion.62 = f32[256,2048]{1,0:T(8,128)S(1)} fusion(bf16[256,2048]{1,0:T(8,128)(2,1)S(1)} %get-tuple-element.411, bf16[2048,6145]{1,0:T(8,128)(2,1)} %all-gather.8.cloned.1.call-done), kind=kOutput, calls=%fused_computation.71 | convolution fusion | flops 2147483648 | bytes 11534336 | tf_op jit(solution)/shard_map/tf,df->td/dot_general | solution.py:224
  334.0 7.7 fusion.80
  341.9 45.2 %all-reduce.7.cloned.1.call-done = bf16[256,2048]{1,0:T(8,128)(2,1)} async-done(((bf16[256,2048]{1,0:T(8,128)(2,1)}), bf16[256,2048]{1,0:T(8,128)(2,1)}) %all-reduce.7.cloned.1.call-update) | async-done | bytes 1048592 | tf_op jit(solution)/shard_map/psum | solution.py:221
  387.0 2.6 fusion.96
  389.7 4.0 fusion.103
  395.2 39.7 %while.31 = (s32[]{:T(128)}, f32[256,8,64]{0,2,1:T(8,128)}, bf16[4,512,8,64]{1,3,2,0:T(8,128)(2,1)}, bf16[4,512,8,64]{1,3,2,0:T(8,128)(2,1)}, bf16[4,512,8,64]{1...) while((s32[]{:T(128)}, f32[256,8,64]{0,2,1:T(8,128)}, ...), condition=%wide.region_12.13_spmd.clone, body=%wide.region_11.12_spmd.clone.sunk | while | flops 685375744 | bytes 63905188 | solution.py:270
  396.4 2.9 fusion.204
  406.3 2.9 fusion.204
  416.2 2.9 fusion.204
  426.2 2.9 fusion.204
  437.4 2.3 pad_maximum_fusion
  441.0 7.5 fusion.84
  448.5 30.1 %reduce-scatter.10.cloned.1.call-done = bf16[256,16,64]{0,2,1:T(8,128)(2,1)} async-done(((bf16[2048,16,64]{0,2,1:T(8,128)(2,1)}), bf16[256,16,64]{0,2,1:T(8,128)(2,1)}) %reduce-scatter.10.cloned.1.call-update) | async-done | bytes 524304 | tf_op jit(solution)/shard_map/reduce_scatter | solution.py:57
  480.0 3.2 fusion.106
  483.2 3.1 convolution_add_fusion.1
  486.4 4.1 fusion.83
  492.0 3.9 convolution_convert_fusion.6
  496.0 6.9 convolution_convert_fusion
  506.1 2.2 convolution_convert_fusion.3
  510.5 38.0 %all-reduce.9.cloned.1.call-done = (bf16[256,2048]{1,0:T(8,128)(2,1)}, bf16[256,2048]{1,0:T(8,128)(2,1)}) async-done(((bf16[256,2048]{1,0:T(8,128)(2,1)}, bf16[256,2048]{1,0:T(8,128)(2,1)}), (bf16[256,2048]{1,0:T(8,128)(2,1)}, bf16[256,2048]{1,0:T(8,128)(2,1)})) %all-reduce.9.cloned.1.call-update) | async-done | bytes 2097168 | tf_op jit(solution)/shard_map/psum | solution.py:306
  550.5 36.8 %concatenate.42 = bf16[2048,1537]{0,1:T(8,128)(2,1)} concatenate(bf16[2048,1]{0,1:T(2,128)(2,1)S(1)} %convert_element_type.242, bf16[2048,512]{0,1:T(8,128)(2,1)} %convolution_convert_fusion.5, bf16[2048,512]{0,1:T(8,128)(2,1)} %convolution_convert_fusion.4, bf16[2048,512]{0,1:T(8,128)(2,1)} %convolution_convert_fusion.3), dimensions={1} | concatenate | bytes 12591104 | tf_op jit(solution)/shard_map/concatenate | solution.py:41
  587.3 9.5 %copy.99 = bf16[2048,1537]{1,0:T(8,128)(2,1)} copy(bf16[2048,1537]{0,1:T(8,128)(2,1)} %concatenate.42) | data formatting | bytes 12591104
  598.2 7.0 convolution_convert_fusion.2
  605.2 5.6 convolution_convert_fusion.1
  610.8 82.3 %concatenate.43 = bf16[2048,4097]{0,1:T(8,128)(2,1)} concatenate(bf16[2048,1]{0,1:T(2,128)(2,1)S(1)} %convert_element_type.254, bf16[2048,2048]{0,1:T(8,128)(2,1)} %convolution_convert_fusion.2, bf16[2048,2048]{0,1:T(8,128)(2,1)} %convolution_convert_fusion.1), dimensions={1} | concatenate | bytes 33562624 | tf_op jit(solution)/shard_map/concatenate | solution.py:41
  693.0 21.5 %copy.101 = bf16[2048,4097]{1,0:T(8,128)(2,1)} copy(bf16[2048,4097]{0,1:T(8,128)(2,1)} %concatenate.43) | data formatting | bytes 33562624
  716.1 4.9 fusion.92
  721.0 6.5 reduce-scatter.14.cloned.1.call-done
  729.2 88.3 %reduce-scatter.16.cloned.1.call-done = bf16[64,1537]{1,0:T(8,128)(2,1)} async-done(((bf16[2048,1537]{1,0:T(8,128)(2,1)}), bf16[64,1537]{1,0:T(8,128)(2,1)}) %reduce-scatter.16.cloned.1.call-update) | async-done | bytes 196752
  822.6 116.0 %reduce-scatter.18.cloned.1.call-done = bf16[64,4097]{1,0:T(8,128)(2,1)} async-done(((bf16[2048,4097]{1,0:T(8,128)(2,1)}), bf16[64,4097]{1,0:T(8,128)(2,1)}) %reduce-scatter.18.cloned.1.call-update) | async-done | bytes 524432
  (276 shorter events, 87.3 us)
Async XLA Ops:
  7.2 61.8 %copy-start = (bf16[256,2048]{1,0:T(8,128)(2,1)S(1)}, bf16[256,2048]{1,0:T(8,128)(2,1)}, u32[]{:S(2)}) copy-start(bf16[256,2048]{1,0:T(8,128)(2,1)} %param.17) | copy-start | bytes 3145732
  7.2 60.5 %all-gather.4.cloned.1.call-start = ((), (), s32[]{:S(2)}) async-start(), calls=%async_computation.5 | async-start | bytes 9191424 | tf_op jit(solution)/shard_map/all_gather | solution.py:20
  10.0 106.1 %all-gather.6.cloned.1.call-start = ((), (), s32[]{:S(2)}) async-start(), calls=%async_computation.6 | async-start | bytes 4718592 | tf_op jit(solution)/shard_map/all_gather | solution.py:36
  79.4 1.6 copy-start.31
  80.4 114.1 %all-reduce.5.cloned.1.call-start = ((), (), s32[]{:S(2)}) async-start(), calls=%async_computation.7 | async-start | bytes 2097152 | tf_op jit(solution)/shard_map/psum | solution.py:197
  143.5 4.2 copy-start.33
  147.6 144.2 %all-gather.8.cloned.1.call-start = ((), (), s32[]{:S(2)}) async-start(), calls=%async_computation.8 | async-start | bytes 26492928 | tf_op jit(solution)/shard_map/all_gather | solution.py:20
  150.3 236.8 %all-reduce.7.cloned.1.call-start = ((), (), s32[]{:S(2)}) async-start(), calls=%async_computation.9 | async-start | bytes 2097152 | tf_op jit(solution)/shard_map/psum | solution.py:221
  294.8 13.6 %copy-start.6 = (bf16[256,2048]{1,0:T(8,128)(2,1)}, bf16[256,2048]{1,0:T(8,128)(2,1)S(1)}, u32[]{:S(2)}) copy-start(bf16[256,2048]{1,0:T(8,128)(2,1)S(1)} %multiply_convert_fusion.3) | copy-start | bytes 3145732
  294.8 7.0 copy-start.8
  317.0 17.0 %copy-start.26 = (bf16[256,2048]{1,0:T(8,128)(2,1)}, bf16[256,2048]{1,0:T(8,128)(2,1)S(1)}, u32[]{:S(2)}) copy-start(bf16[256,2048]{1,0:T(8,128)(2,1)S(1)} %get-tuple-element.411) | copy-start | bytes 3145732
  317.0 17.0 %copy-start.28 = (bf16[256,2048]{1,0:T(8,128)(2,1)}, bf16[256,2048]{1,0:T(8,128)(2,1)S(1)}, u32[]{:S(2)}) copy-start(bf16[256,2048]{1,0:T(8,128)(2,1)S(1)} %get-tuple-element.410) | copy-start | bytes 3145732
  341.8 136.9 %reduce-scatter.10.cloned.1.call-start = ((), (), s32[]{:S(2)}) async-start(), calls=%async_computation.10 | async-start | bytes 4718592 | tf_op jit(solution)/shard_map/reduce_scatter | solution.py:57
  387.0 2.6 copy-start.4
  387.0 2.7 copy-start.9
  387.0 2.7 copy-start.12
  389.7 4.0 copy-start.24
  396.4 2.9 copy-start.17
  400.6 3.1 copy-start.18
  400.6 2.3 copy-start.19
  403.7 1.4 copy-start.20
  406.3 2.9 copy-start.17
  409.2 1.3 copy-start.1
  410.5 3.1 copy-start.18
  410.5 2.3 copy-start.19
  413.7 1.4 copy-start.20
  416.2 2.9 copy-start.17
  420.4 3.1 copy-start.18
  420.5 2.3 copy-start.19
  423.6 1.4 copy-start.20
  426.2 2.9 copy-start.17
  430.4 3.1 copy-start.18
  430.4 2.3 copy-start.19
  433.5 1.4 copy-start.20
  434.9 2.2 copy-start.21
  439.8 108.7 %all-reduce.9.cloned.1.call-start = ((), (), s32[]{:S(2)}) async-start(), calls=%async_computation.15 | async-start | bytes 4194304 | tf_op jit(solution)/shard_map/psum | solution.py:306
  441.0 38.8 %copy-start.3 = (f32[256,8,64]{0,2,1:T(8,128)S(1)}, f32[256,8,64]{0,2,1:T(8,128)}, u32[]{:S(2)}) copy-start(f32[256,8,64]{0,2,1:T(8,128)} %get-tuple-element.147) | copy-start | bytes 1572868
  479.8 6.6 copy-start.15
  480.0 3.2 copy-start.13
  490.5 1.5 copy-start.10
  490.5 224.0 %reduce-scatter.12.cloned.1.call-start = ((), (), s32[]{:S(2)}) async-start(), calls=%async_computation.11 | async-start | bytes 2162688 | tf_op jit(solution)/shard_map/reduce_scatter | solution.py:325
  496.0 231.5 %reduce-scatter.14.cloned.1.call-start = ((), (), s32[]{:S(2)}) async-start(), calls=%async_computation.12 | async-start | bytes 8650752 | tf_op jit(solution)/shard_map/reduce_scatter | solution.py:245
  503.0 3.1 copy-start.16
  503.0 314.6 %reduce-scatter.16.cloned.1.call-start = ((), (), s32[]{:S(2)}) async-start(), calls=%async_computation.13 | async-start | bytes 7028736
  596.8 1.3 copy-start.7
  596.9 341.8 %reduce-scatter.18.cloned.1.call-start = ((), (), s32[]{:S(2)}) async-start(), calls=%async_computation.14 | async-start | bytes 17842176
  598.2 7.0 copy-start.27
  714.5 1.6 copy-start.11
  (27 other events, 26.1 us)
Sparse Core Ops, SparseCore 0:
  10.8 56.7 all-gather.3
  80.5 35.4 all-gather.5
  147.7 46.7 all-reduce.4
  197.5 94.3 all-gather.7
  341.9 45.0 all-reduce.6
  439.9 38.7 reduce-scatter.9
  490.6 57.7 all-reduce.8
  552.4 78.7 reduce-scatter.11
  635.4 92.0 reduce-scatter.13
  731.1 86.4 reduce-scatter.15
  822.0 116.5 reduce-scatter.17
where the time goes:
time: 966 us; the launch traced here: 951 us
  waiting for transfers between devices  554 us (57%)
  local copies, waits for them, and re-layouts  194 us (20%)
  matrix products  151 us (16%)
  other arithmetic  35.8 us (4%)
  between operations  14.9 us (2%)
    unnamed x13, waiting for transfers between devices  205 us
    all_gather x2, waiting for transfers between devices, gather_turned(): whole = lax.all_gather(both, axis, axis=0, tiled=True)  151 us
    concatenate x2, local copies, waits for them, and re-layouts, in_one_piece(): both = jnp.concatenate(columns, axis=along)  119 us
    psum x1, waiting for transfers between devices, body(): lax.psum((jnp.einsum('tf,df->td', d_gate, gate_full, preferred_element_ty...  45.2 us
    psum x1, waiting for transfers between devices, body(): lax.psum(jnp.dot(attended_low, o_full, preferred_element_type=jnp.float32...  44 us
    unnamed x64, local copies, waits for them, and re-layouts  43.9 us
    psum x1, waiting for transfers between devices, body(): lax.psum(d_normed_one.astype(jnp.bfloat16), 'tensor').astype(jnp.float32)  38 us
    all_gather x1, waiting for transfers between devices, sent_together(): lax.all_gather(both, axis, axis=dim, tiled=True)  34.3 us
  transfers between devices with their start and end apart: 11, of which 10 were waited for; matrix products, arithmetic and copies ran while one was open for 22% of the time, Pallas kernels for 0%

commit v1 on v0

v1 whole, which is shorter than its diff:
```python
import jax
import jax.numpy as jnp
from jax import lax
from jax.experimental import pallas as pl
from jax.experimental.pallas import tpu as pltpu
from jax.sharding import Mesh
from jax.sharding import PartitionSpec as P

HEAD_DIM = 64
BLOCK = 512

epsilon = 1e-05
rope_base = 130000.0
masked_low = -1000000000.0

f32 = jnp.float32
bf16 = jnp.bfloat16
MESH = pl.DeviceIdType.MESH
VMEM = pl.BlockSpec(memory_space=pltpu.VMEM)
HBM = pl.BlockSpec(memory_space=pl.ANY)


def dot_nn(a, b):
    return lax.dot_general(a, b, (((1,), (0,)), ((), ())), preferred_element_type=f32)


def dot_nt(a, b):
    return lax.dot_general(a, b, (((1,), (1,)), ((), ())), preferred_element_type=f32)


def dot_tn(a, b):
    return lax.dot_general(a, b, (((0,), (0,)), ((), ())), preferred_element_type=f32)


def place():
    return tuple(lax.axis_index(a) for a in ("shard", "x", "core", "tensor"))


def turned(index, step):
    return lax.rem(index + step, 4)


def on_axis(axis, index):
    return {axis: index}


def meet(axes):
    barrier = pltpu.get_barrier_semaphore()
    count = 0
    for axis in axes:
        me = lax.axis_index(axis)
        peers = [1 - me] if axis == "core" else [turned(me, d) for d in (1, 2, 3)]
        for peer in peers:
            pl.semaphore_signal(barrier, inc=1, device_id={axis: peer}, device_id_type=MESH)
            count += 1
    pl.semaphore_wait(barrier, count)


def remote(src, dst, send, recv, axis, index):
    return pltpu.make_async_remote_copy(
        src_ref=src, dst_ref=dst, send_sem=send, recv_sem=recv, device_id={axis: index}, device_id_type=MESH
    )


def gather_kernel(
    wq, wk, wv, wo, gains, tokens, cot, table,
    full, gain_all, chip_tokens, chip_cot, chip_table, normed, gain_rows,
    local, core_send, core_recv, send, recv, gain_send, gain_recv,
):
    z, x, core, y = place()
    half = wq.shape[1] // 2
    rows = wq.shape[0]
    meet(("core", "x", "shard"))
    at = pl.ds(pl.multiple_of(core * rows, rows), rows)
    keep = pl.ds(pl.multiple_of(core * half, half), half)
    give = pl.ds(pl.multiple_of((1 - core) * half, half), half)
    inside, across = [], []
    pairs = [(gains, gains, gain_all.at[z, x, core])]
    for k, w in enumerate((wq, wk, wv, wo)):
        pairs.append((w.at[:, keep], w.at[:, give], full.at[z, x, at, pl.ds(k * half, half)]))
    pairs += [(a, a, b.at[core]) for a, b in ((tokens, chip_tokens), (table, chip_table), (cot, chip_cot))]
    for k, (mine, theirs, there) in enumerate(pairs):
        inside.append(pltpu.make_async_copy(mine, there, local.at[k]))
        across.append(remote(theirs, there, core_send.at[k], core_recv.at[k], "core", 1 - core))
        across[-1].start()
        inside[-1].start()

    def arrived(ks):
        for k in ks:
            inside[k].wait()
            across[k].wait_recv()

    first, second = pl.ds(0, 2 * half), pl.ds(2 * half, 2 * half)
    started = []

    def spread(src, dst, s, r, axis, me, k):
        for d in (1, 2, 3):
            copy = remote(src, dst, s.at[k, d - 1], r.at[k, d - 1], axis, turned(me, d))
            copy.start()
            started.append(copy)

    arrived((0,))
    spread(gain_all.at[z, x], gain_all.at[z, x], gain_send, gain_recv, "x", x, 0)
    arrived((1, 2))
    spread(full.at[z, x, :, first], full.at[z, x, :, first], send, recv, "x", x, 0)
    arrived((3, 4))
    spread(full.at[z, x, :, second], full.at[z, x, :, second], send, recv, "shard", z, 1)
    for copy in started[0:3]:
        copy.wait_recv()
    spread(gain_all.at[z], gain_all.at[z], gain_send, gain_recv, "shard", z, 1)
    for copy in started[3:6]:
        copy.wait_recv()
    spread(full.at[z, :, :, first], full.at[z, :, :, first], send, recv, "shard", z, 2)
    for copy in started[6:9]:
        copy.wait_recv()
    spread(full.at[:, x, :, second], full.at[:, x, :, second], send, recv, "x", x, 3)
    for copy in started[9:12]:
        copy.wait_recv()
    for i in range(16):
        two = (gain_all[i // 4, i % 4, 0] + gain_all[i // 4, i % 4, 1]).astype(f32)
        gain_rows[:, pl.ds(i * 128, 128)] = two[0:8, :]
    arrived((5, 6, 7))

    def norm(i, unused):
        values = chip_tokens[i // 4, pl.ds(pl.multiple_of(lax.rem(i, 4) * 64, 64), 64), :].astype(f32)
        scale = lax.rsqrt(jnp.mean(values * values, axis=-1, keepdims=True) + epsilon)
        normed[pl.ds(pl.multiple_of(i * 64, 64), 64), :] = ((values * scale) * gain_rows[0:1, :]).astype(bf16)
        return unused

    lax.fori_loop(0, 8, norm, 0)
    for copy in started[12:]:
        copy.wait_recv()
    for copy in across + started:
        copy.wait_send()


def gather_attention(wq, wk, wv, wo, gains, tokens, cot, table):
    rows, width = tokens.shape
    sds = jax.ShapeDtypeStruct
    dma = pltpu.SemaphoreType.DMA
    return pl.pallas_call(
        gather_kernel,
        out_shape=(
            sds((4, 4, 128, 2 * wq.shape[1]), bf16),
            sds((4, 4, 2, 16, 128), bf16),
            sds((2, rows, width), bf16),
            sds((2, rows, width), bf16),
            sds((2, rows, 128), f32),
            sds((2 * rows, width), bf16),
            sds((8, width), f32),
        ),
        in_specs=[HBM] * 4 + [VMEM] + [HBM] * 3,
        out_specs=(HBM, VMEM, VMEM, HBM, HBM, VMEM, VMEM),
        scratch_shapes=[dma((8,)), dma((8,)), dma((8,)), dma((4, 3)), dma((4, 3)), dma((2, 3)), dma((2, 3))],
        compiler_params=pltpu.CompilerParams(
            collective_id=0, has_side_effects=True, vmem_limit_bytes=40 << 20
        ),
    )(wq, wk, wv, wo, gains, tokens, cot, table)


def rope(vectors, table_cos, table_sin):
    n = vectors.shape[1]
    lane = lax.broadcasted_iota(jnp.int32, vectors.shape, 1)
    other = jnp.where(
        lax.rem(lane, HEAD_DIM) < HEAD_DIM // 2,
        pltpu.roll(vectors, n - HEAD_DIM // 2, 1),
        pltpu.roll(vectors, HEAD_DIM // 2, 1),
    )
    return vectors * table_cos + other * table_sin


def masked(raw, begin, j, i):
    key = lax.broadcasted_iota(jnp.int32, raw.shape, 0) + j * BLOCK
    query = lax.broadcasted_iota(jnp.int32, raw.shape, 1) + i * BLOCK
    return jnp.where((key >= begin) & (key <= query), raw * HEAD_DIM ** (-0.5), masked_low)


def sum_and_share(c, y, own, other, pair, near, out, mid_of, csem, ysem, asem, fsem):
    started = []
    for d in (2, 1, 3, 0):
        k = turned(y, d)
        copy = remote(other.at[k], pair.at[k], csem.at[0, d], csem.at[1, d], "core", 1 - c)
        copy.start()
        started.append(copy)
    arrive = dict(zip((2, 1, 3, 0), started))
    ysent = {}
    for d in (2, 1, 3):
        k = turned(y, d)
        arrive[d].wait_recv()
        arrive[d].wait_send()
        other[k] = (own[k] + pair[k].astype(f32)).astype(bf16)
        ysent[d] = remote(other.at[k], near.at[d - 1], ysem.at[0, d - 1], ysem.at[1, d - 1], "tensor", k)
        ysent[d].start()
    arrive[0].wait_recv()
    arrive[0].wait_send()
    total = own[y] + pair[y].astype(f32)
    for d in (1, 3, 2):
        ysent[d].wait_recv()
        total = total + near[d - 1].astype(f32)
    mid_of(total)
    share = {}
    for d in (2, 1, 3):
        share[d] = remote(out.at[c, y], out.at[c, y], asem.at[0, d - 1], asem.at[1, d - 1], "tensor", turned(y, d))
        share[d].start()
    forward = [remote(out.at[c, y], out.at[c, y], fsem.at[0, 0], fsem.at[1, 0], "core", 1 - c)]
    forward[0].start()
    for d in (1, 3, 2):
        share[d].wait_recv()
        k = turned(y, 4 - d)
        forward.append(remote(out.at[c, k], out.at[c, k], fsem.at[0, d], fsem.at[1, d], "core", 1 - c))
        forward[-1].start()
    for copy in forward:
        copy.wait_recv()
    for copy in [*ysent.values(), *share.values(), *forward]:
        copy.wait_send()


def forward_kernel(
    normed, weights, table, start, tokens, gain_rows,
    qkv_out, low, attended_out, lse, middle, normed_two,
    packed, arrived, value_t, head_out, low_in, own, other, pair, near,
    xsem, lsem, csem, ysem, asem, fsem,
):
    z, x, c, y = place()
    meet(("core", "x", "tensor"))
    chip = normed.shape[0]
    wide = 4 * HEAD_DIM
    cosine = jnp.concatenate([table[:, 0:64]] * 4, axis=1)
    sine = jnp.concatenate([table[:, 64:128]] * 4, axis=1)
    queries = rope(dot_nn(normed[...], weights[:, 0:wide]), cosine, sine).astype(bf16)
    keys = rope(dot_nn(normed[...], weights[:, wide : 2 * wide]), cosine, sine).astype(bf16)
    for h in range(4):
        lanes = slice(h * HEAD_DIM, (h + 1) * HEAD_DIM)
        packed[h, 0:chip, :] = jnp.concatenate([queries[:, lanes], keys[:, lanes]], axis=1)
    values = dot_nn(normed[...], weights[:, 2 * wide : 3 * wide]).astype(bf16)
    for h in range(4):
        lanes = slice(h * HEAD_DIM, (h + 1) * HEAD_DIM)
        packed[h, chip:, :] = jnp.concatenate(
            [values[0 : chip // 2, lanes], values[chip // 2 :, lanes]], axis=1
        )
    sent = []
    for d in (2, 1, 3):
        k = turned(x, d)
        sent.append(remote(packed.at[k], arrived.at[x], xsem.at[0, d - 1], xsem.at[1, d - 1], "x", k))
        sent[-1].start()
    arrived[x] = packed[x]
    for copy in sent:
        copy.wait_recv()
    for k in range(4):
        rows = slice(k * chip, (k + 1) * chip)
        qkv_out[0, rows, :] = arrived[k, 0:chip, 0:64]
        qkv_out[1, rows, :] = arrived[k, 0:chip, 64:128]
        block = jnp.concatenate([arrived[k, chip:, 0:64], arrived[k, chip:, 64:128]], axis=0)
        qkv_out[2, rows, :] = block
        value_t[:, rows] = jnp.transpose(block)
    low_sent = []
    for i in range(4):
        at = slice(i * BLOCK, (i + 1) * BLOCK)
        begin = start[:, at]
        mine = qkv_out[0, at, :]

        def step(j, state):
            peak, total, summed = state
            key_at = pl.ds(pl.multiple_of(j * BLOCK, BLOCK), BLOCK)
            scores = masked(dot_nt(qkv_out[1, key_at, :], mine), begin, j, i)
            new = jnp.maximum(peak, jnp.max(scores, axis=0, keepdims=True))
            weight = jnp.exp(scores - new)
            factor = jnp.exp(peak - new)
            total = total * factor + jnp.sum(weight, axis=0, keepdims=True)
            summed = summed * factor + dot_nn(value_t[:, key_at], weight.astype(bf16))
            return (new, total, summed)

        state = (
            jnp.full((1, BLOCK), masked_low, f32),
            jnp.zeros((1, BLOCK), f32),
            jnp.zeros((HEAD_DIM, BLOCK), f32),
        )
        state = step(i, state)
        peak, total, summed = lax.fori_loop(0, i, step, state) if i else state
        attended = jnp.transpose(summed / total)
        attended_out[at, :] = attended
        lse[:, at] = peak + jnp.log(total)
        head_out[i] = attended.astype(bf16)

        @pl.when(x != i)
        def send(i=i):
            remote(head_out.at[i], low_in.at[x], lsem.at[0, i], lsem.at[1, x], "x", i).start()

    low_in[x] = head_out[x]
    for d in (1, 2, 3):
        k = turned(x, d)
        copy = remote(head_out.at[k], low_in.at[k], lsem.at[0, k], lsem.at[1, k], "x", k)
        copy.wait_recv()
        copy.wait_send()
    low[...] = jnp.concatenate([low_in[h] for h in range(4)], axis=1)
    half = chip // 2
    quarter = half // 4
    out_weights = weights[:, 3 * wide : 4 * wide]
    theirs = low[pl.ds(pl.multiple_of((1 - c) * half, half), half), :]
    other[...] = dot_nt(theirs, out_weights).astype(bf16).reshape(other.shape)
    mine = low[pl.ds(pl.multiple_of(c * half, half), half), :]
    own[...] = dot_nt(mine, out_weights).reshape(own.shape)

    def finish(total):
        row = tokens[c, pl.ds(pl.multiple_of(y * quarter, quarter), quarter), :].astype(f32)
        mid = row + total
        middle[...] = mid
        scale = lax.rsqrt(jnp.mean(mid * mid, axis=-1, keepdims=True) + epsilon)
        normed_two[c, y] = ((mid * scale) * gain_rows[1:2, :]).astype(bf16)

    sum_and_share(c, y, own, other, pair, near, normed_two, finish, csem, ysem, asem, fsem)
    for copy in sent:
        copy.wait_send()


def attention_forward(normed, weights, table, start, tokens, gain_rows):
    chip, width = normed.shape
    seq = start.shape[1]
    sds = jax.ShapeDtypeStruct
    dma = pltpu.SemaphoreType.DMA
    quarter = chip // 8
    return pl.pallas_call(
        forward_kernel,
        out_shape=(
            sds((3, seq, HEAD_DIM), bf16),
            sds((chip, 4 * HEAD_DIM), bf16),
            sds((seq, HEAD_DIM), f32),
            sds((1, seq), f32),
            sds((quarter, width), f32),
            sds((2, 4, quarter, width), bf16),
        ),
        in_specs=[VMEM] * 6,
        out_specs=(VMEM,) * 6,
        scratch_shapes=[
            pltpu.VMEM((4, chip * 3 // 2, 128), bf16),
            pltpu.VMEM((4, chip * 3 // 2, 128), bf16),
            pltpu.VMEM((HEAD_DIM, seq), bf16),
            pltpu.VMEM((4, chip, HEAD_DIM), bf16),
            pltpu.VMEM((4, chip, HEAD_DIM), bf16),
            pltpu.VMEM((4, quarter, width), f32),
            pltpu.VMEM((4, quarter, width), bf16),
            pltpu.VMEM((4, quarter, width), bf16),
            pltpu.VMEM((3, quarter, width), bf16),
            dma((2, 3)), dma((2, 4)), dma((2, 4)), dma((2, 3)), dma((2, 3)), dma((2, 4)),
        ],
        compiler_params=pltpu.CompilerParams(
            collective_id=1, has_side_effects=True, vmem_limit_bytes=56 << 20
        ),
    )(normed, weights, table, start, tokens, gain_rows)


def mlp_kernel(
    normed, cot, gate_w, up_w, down_w, mixed, d_normed, grads, normed_t, cot_t, mixed_sum, d_sum
):
    step = pl.program_id(0)

    @pl.when(step == 0)
    def first():
        normed_t[...] = jnp.transpose(normed[...])
        cot_t[...] = jnp.transpose(cot[...])
        mixed_sum[...] = jnp.zeros_like(mixed_sum)
        d_sum[...] = jnp.zeros_like(d_sum)

    gate = dot_nn(normed[...], gate_w[...])
    upper = dot_nn(normed[...], up_w[...])
    d_hidden = dot_nn(cot[...], down_w[...])
    sigmoid = 1.0 / (1.0 + jnp.exp(-gate))
    silu = gate * sigmoid
    hidden = (silu * upper).astype(bf16)
    d_gate = (d_hidden * upper * (sigmoid * (1.0 + gate * (1.0 - sigmoid)))).astype(bf16)
    d_upper = (d_hidden * silu).astype(bf16)
    for k, (left, right) in enumerate(((normed_t, d_gate), (normed_t, d_upper), (cot_t, hidden))):
        grads[:, k] = dot_nn(left[...], right).astype(bf16).reshape(grads.shape[0], *grads.shape[2:])
    d_sum[...] += dot_nt(d_gate, gate_w[...]) + dot_nt(d_upper, up_w[...])
    mixed_sum[...] += dot_nt(hidden, down_w[...])

    @pl.when(step == pl.num_programs(0) - 1)
    def last():
        mixed[...] = mixed_sum[...].astype(bf16)
        d_normed[...] = d_sum[...].astype(bf16)


def mlp(normed, cot, full):
    chip, width = normed.shape
    ff = full.shape[1] // 3
    chunk = 256
    steps = ff // chunk
    sds = jax.ShapeDtypeStruct
    piece = [
        pl.BlockSpec((width, chunk), lambda f, k=k: (0, k * steps + f)) for k in range(3)
    ]
    return pl.pallas_call(
        mlp_kernel,
        grid=(steps,),
        out_shape=(
            sds((chip, width), bf16),
            sds((chip, width), bf16),
            sds((16, 3, width // 16, ff), bf16),
        ),
        in_specs=[VMEM, VMEM, *piece],
        out_specs=(VMEM, VMEM, pl.BlockSpec((16, 3, width // 16, chunk), lambda f: (0, 0, 0, f))),
        scratch_shapes=[
            pltpu.VMEM((width, chip), bf16),
            pltpu.VMEM((width, chip), bf16),
            pltpu.VMEM((chip, width), f32),
            pltpu.VMEM((chip, width), f32),
        ],
        compiler_params=pltpu.CompilerParams(vmem_limit_bytes=60 << 20),
        cost_estimate=pl.CostEstimate(flops=20 << 30, bytes_accessed=30 << 20, transcendentals=1 << 20),
    )(normed, cot, full, full, full)


def backward_kernel(
    d_part, mix_part, middle, own_tokens, own_cot, gain_rows, weights, low, normed, qkv, attended, lse, start, table,
    layer_out, input_grad, grads, gain_out,
    d_branch, d_mid, pair, half_sum, near, heads, head_in, key_t, d_key, d_value, packed, arrived, partial,
    turned_rows, terms, wide_in, wide_sum, thin_in, thin_sum, gain_part, gain_y, gain_c, gain_x, gain_z,
    csem, ysem, asem, fsem, hsem, psem, wsem, tsem, gsem, outsem,
):
    z, x, c, y = place()
    meet(("core", "x", "tensor", "shard"))
    chip, width = normed.shape
    half, quarter = chip // 2, chip // 8
    wide = 4 * HEAD_DIM
    waits = []

    def begin(copy):
        copy.start()
        waits.append(copy)
        return copy

    def cross(r, part):
        return {
            d: begin(remote(part.at[1 - c, turned(y, d)], pair.at[r, turned(y, d)], csem.at[r, 0, d], csem.at[r, 1, d], "core", 1 - c))
            for d in (2, 1, 3, 0)
        }

    def along(r, part, crossed):
        sent = {}
        for d in (2, 1, 3):
            k = turned(y, d)
            crossed[d].wait_recv()
            half_sum[r, k] = (part[c, k].astype(f32) + pair[r, k].astype(f32)).astype(bf16)
            sent[d] = begin(remote(half_sum.at[r, k], near.at[r, d - 1], ysem.at[r, 0, d - 1], ysem.at[r, 1, d - 1], "tensor", k))
        return sent

    def total_of(r, part, crossed, sent):
        crossed[0].wait_recv()
        total = part[c, y].astype(f32) + pair[r, y].astype(f32)
        for d in (1, 3, 2):
            sent[d].wait_recv()
            total = total + near[r, d - 1].astype(f32)
        return total

    def share(r, slot):
        return {
            d: begin(remote(slot, slot, asem.at[r, 0, d - 1], asem.at[r, 1, d - 1], "tensor", turned(y, d)))
            for d in (2, 1, 3)
        }

    d_crossed = cross(0, d_part)
    m_crossed = cross(1, mix_part)
    d_sent = along(0, d_part, d_crossed)
    mid = middle[...]
    scale = lax.rsqrt(jnp.mean(mid * mid, axis=-1, keepdims=True) + epsilon)
    unit = mid * scale
    d_two = total_of(0, d_part, d_crossed, d_sent)
    gain_two_part = jnp.sum(d_two * unit, axis=0, keepdims=True)
    scaled = d_two * gain_rows[1:2, :]
    d_middle = own_cot[...].astype(f32) + scale * (
        scaled - unit * jnp.mean(scaled * unit, axis=-1, keepdims=True)
    )
    d_mid[...] = d_middle
    d_branch[c, y] = d_middle.astype(bf16)
    shared = share(0, d_branch.at[c, y])
    forward = [begin(remote(d_branch.at[c, y], d_branch.at[c, y], fsem.at[0, 0], fsem.at[1, 0], "core", 1 - c))]
    m_sent = along(1, mix_part, m_crossed)
    for d in (1, 3, 2):
        shared[d].wait_recv()
        k = turned(y, 4 - d)
        forward.append(begin(remote(d_branch.at[c, k], d_branch.at[c, k], fsem.at[0, d], fsem.at[1, d], "core", 1 - c)))
    for copy in forward:
        copy.wait_recv()
    branch = d_branch[...].reshape(chip, width)
    d_heads = dot_nn(branch, weights[:, 3 * wide : 4 * wide]).astype(bf16)
    for h in range(4):
        heads[h] = d_heads[:, h * HEAD_DIM : (h + 1) * HEAD_DIM]
    head_sent = {}
    for d in (2, 1, 3):
        k = turned(x, d)
        head_sent[d] = begin(remote(heads.at[k], head_in.at[x], hsem.at[0, d - 1], hsem.at[1, d - 1], "x", k))
    head_in[x] = heads[x]
    layer_out[y] = (mid + total_of(1, mix_part, m_crossed, m_sent)).astype(bf16)
    out_shared = share(1, layer_out.at[y])
    turned_rows[...] = jnp.transpose(branch)
    terms[:, :, 3 * wide : 4 * wide] = (
        dot_nn(turned_rows[...], low[...]).astype(bf16).reshape(16, width // 16, wide)
    )
    for k in range(4):
        rows = slice(k * chip, (k + 1) * chip)
        key_t[:, rows] = jnp.transpose(qkv[1, rows, :])
    d_key[...] = jnp.zeros_like(d_key)
    d_value[...] = jnp.zeros_like(d_value)
    for d in (1, 3, 2):
        head_sent[d].wait_recv()

    for i in (3, 2, 1, 0):
        at = slice(i * BLOCK, (i + 1) * BLOCK)
        mine, d_out = qkv[0, at, :], head_in[i]
        product = d_out.astype(f32) * attended[at, :]
        center = jnp.sum(jnp.transpose(product), axis=0, keepdims=True)
        peak, first = lse[:, at], start[:, at]

        def step(j, d_query):
            key_at = pl.ds(pl.multiple_of(j * BLOCK, BLOCK), BLOCK)
            weight = jnp.exp(masked(dot_nt(qkv[1, key_at, :], mine), first, j, i) - peak)
            d_prob = dot_nt(qkv[2, key_at, :], d_out)
            d_raw = (weight * (d_prob - center) * HEAD_DIM ** (-0.5)).astype(bf16)
            d_key[key_at, :] += dot_nn(d_raw, mine)
            d_value[key_at, :] += dot_nn(weight.astype(bf16), d_out)
            return d_query + dot_nn(key_t[:, key_at], d_raw)

        d_query = lax.fori_loop(0, i + 1, step, jnp.zeros((HEAD_DIM, BLOCK), f32))
        packed[i, 0:chip, :] = jnp.concatenate(
            [jnp.transpose(d_query).astype(bf16), d_key[at, :].astype(bf16)], axis=1
        )
        d_rows = d_value[at, :].astype(bf16)
        packed[i, chip:, :] = jnp.concatenate([d_rows[0:half], d_rows[half:]], axis=1)

        @pl.when(x != i)
        def send(i=i):
            remote(packed.at[i], arrived.at[x], psem.at[0, i], psem.at[1, x], "x", i).start()

    arrived[x] = packed[x]
    turned_rows[...] = jnp.transpose(normed[...])
    for d in (1, 2, 3):
        k = turned(x, d)
        copy = remote(packed.at[k], arrived.at[k], psem.at[0, k], psem.at[1, k], "x", k)
        copy.wait_recv()
        waits.append(copy)
    cosine = jnp.concatenate([table[:, 0:64]] * 4, axis=1)
    sine = jnp.concatenate([table[:, 64:128]] * 4, axis=1)

    def side_by_side(lanes):
        return jnp.concatenate([arrived[h, 0:chip, lanes].astype(f32) for h in range(4)], axis=1)

    d_lin = jnp.concatenate(
        [
            rope(side_by_side(slice(0, 64)), cosine, -sine).astype(bf16),
            rope(side_by_side(slice(64, 128)), cosine, -sine).astype(bf16),
            jnp.concatenate(
                [
                    jnp.concatenate([arrived[h, chip:, lanes] for h in range(4)], axis=1)
                    for lanes in (slice(0, 64), slice(64, 128))
                ],
                axis=0,
            ),
        ],
        axis=1,
    )
    terms[:, :, 0 : 3 * wide] = dot_nn(turned_rows[...], d_lin).astype(bf16).reshape(16, width // 16, 3 * wide)

    first, second = pl.ds(0, 2 * wide), pl.ds(2 * wide, 2 * wide)
    wide_sent = {}
    for d in (2, 1, 3):
        kz, kx = turned(z, d), turned(x, d)
        wide_sent[0, d] = begin(remote(terms.at[pl.ds(pl.multiple_of(4 * kz, 4), 4), :, first], wide_in.at[0, d - 1], wsem.at[0, 0, d - 1], wsem.at[0, 1, d - 1], "shard", kz))
        for q in range(4):
            wide_sent[1, d, q] = begin(remote(terms.at[4 * q + kx, :, second], wide_in.at[1, d - 1, q], wsem.at[1 + q, 0, d - 1], wsem.at[1 + q, 1, d - 1], "x", kx))
    lin = [d_lin[0:half], d_lin[half:]]
    for k in range(2):
        partial[k] = dot_nt(lin[k], weights[:, 0 : 3 * wide]).astype(bf16).reshape(4, quarter, width)
    crossed = cross(2, partial)
    sent = along(2, partial, crossed)
    own = own_tokens[...].astype(f32)
    own_scale = lax.rsqrt(jnp.mean(own * own, axis=-1, keepdims=True) + epsilon)
    own_unit = own * own_scale
    d_one = total_of(2, partial, crossed, sent)
    scaled = d_one * gain_rows[0:1, :]
    input_grad[y] = (
        d_mid[...] + own_scale * (scaled - own_unit * jnp.mean(scaled * own_unit, axis=-1, keepdims=True))
    ).astype(bf16)
    in_shared = share(2, input_grad.at[y])
    both = jnp.concatenate(
        [jnp.sum(d_one * own_unit, axis=0, keepdims=True), gain_two_part, jnp.zeros((6, width), f32)], axis=0
    )
    for k in range(16):
        gain_part[k] = both[:, k * 128 : (k + 1) * 128]

    def pass_on(r, src_of, into, axis, me):
        return {
            d: begin(remote(src_of(turned(me, d)), into.at[d - 1], gsem.at[r, 0, d - 1], gsem.at[r, 1, d - 1], axis, turned(me, d)))
            for d in (2, 1, 3)
        }

    moved = pass_on(0, lambda k: gain_part.at[pl.ds(pl.multiple_of(4 * k, 4), 4)], gain_z, "shard", z)
    for d in (1, 3, 2):
        wide_sent[0, d].wait_recv()
    wide_sum[0] = (
        terms[pl.ds(pl.multiple_of(4 * z, 4), 4), :, 0 : 2 * wide].astype(f32)
        + wide_in[0, 0].astype(f32) + wide_in[0, 1].astype(f32) + wide_in[0, 2].astype(f32)
    ).astype(bf16)
    thin_sent = {}
    for d in (2, 1, 3):
        kx = turned(x, d)
        thin_sent[0, d] = begin(remote(wide_sum.at[0, kx], thin_in.at[0, d - 1], tsem.at[0, 0, d - 1], tsem.at[0, 1, d - 1], "x", kx))
    for d in (1, 3, 2):
        for q in range(4):
            wide_sent[1, d, q].wait_recv()
    for q in range(4):
        wide_sum[1, q] = (
            terms[4 * q + x, :, 2 * wide : 4 * wide].astype(f32)
            + wide_in[1, 0, q].astype(f32) + wide_in[1, 1, q].astype(f32) + wide_in[1, 2, q].astype(f32)
        ).astype(bf16)
    for d in (2, 1, 3):
        kz = turned(z, d)
        thin_sent[1, d] = begin(remote(wide_sum.at[1, kz], thin_in.at[1, d - 1], tsem.at[1, 0, d - 1], tsem.at[1, 1, d - 1], "shard", kz))
    for d in (1, 3, 2):
        moved[d].wait_recv()
    gain_part[pl.ds(pl.multiple_of(4 * z, 4), 4)] += gain_z[0] + gain_z[1] + gain_z[2]
    moved = pass_on(1, lambda k: gain_part.at[4 * z + k], gain_x, "x", x)
    for d in (1, 3, 2):
        moved[d].wait_recv()
    gain_y[3] = gain_part[4 * z + x] + gain_x[0] + gain_x[1] + gain_x[2]
    moved = pass_on(2, lambda k: gain_y.at[3], gain_y, "tensor", y)
    for d in (1, 3, 2):
        moved[d].wait_recv()
    gain_c[0] = (gain_y[0] + gain_y[1]) + (gain_y[2] + gain_y[3])
    across = begin(remote(gain_c.at[0], gain_c.at[1], gsem.at[3, 0, 0], gsem.at[3, 1, 0], "core", 1 - c))
    for s, me in ((0, x), (1, z)):
        for d in (1, 3, 2):
            thin_sent[s, d].wait_recv()
        thin_sum[:, s * 2 * wide : (s + 1) * 2 * wide] = (
            wide_sum[s, me].astype(f32)
            + thin_in[s, 0].astype(f32) + thin_in[s, 1].astype(f32) + thin_in[s, 2].astype(f32)
        ).astype(bf16)
    rows = width // 32
    mine = pl.ds(pl.multiple_of(c * rows, rows), rows)
    theirs = pl.ds(pl.multiple_of((1 - c) * rows, rows), rows)
    last = begin(remote(thin_sum.at[theirs], grads.at[c], outsem.at[0], outsem.at[1], "core", 1 - c))
    grads[c] = thin_sum[mine, :]
    across.wait_recv()
    gain_out[...] = gain_c[0] + gain_c[1]
    last.wait_recv()
    for shared in (out_shared, in_shared):
        for d in (1, 3, 2):
            shared[d].wait_recv()
    for copy in waits:
        copy.wait_send()


def attention_backward(
    d_part, mix_part, middle, own_tokens, own_cot, gain_rows, weights, low, normed, qkv, attended, lse, start, table
):
    chip, width = normed.shape
    seq = start.shape[1]
    quarter = chip // 8
    columns = weights.shape[1]
    sds = jax.ShapeDtypeStruct
    dma = pltpu.SemaphoreType.DMA
    vmem = pltpu.VMEM
    return pl.pallas_call(
        backward_kernel,
        out_shape=(
            sds((4, quarter, width), bf16),
            sds((4, quarter, width), bf16),
            sds((2, width // 32, columns), bf16),
            sds((8, 128), f32),
        ),
        in_specs=[VMEM] * 14,
        out_specs=(VMEM,) * 4,
        scratch_shapes=[
            vmem((2, 4, quarter, width), bf16),
            vmem((quarter, width), f32),
            vmem((3, 4, quarter, width), bf16),
            vmem((3, 4, quarter, width), bf16),
            vmem((3, 3, quarter, width), bf16),
            vmem((4, chip, HEAD_DIM), bf16),
            vmem((4, chip, HEAD_DIM), bf16),
            vmem((HEAD_DIM, seq), bf16),
            vmem((seq, HEAD_DIM), f32),
            vmem((seq, HEAD_DIM), f32),
            vmem((4, chip * 3 // 2, 128), bf16),
            vmem((4, chip * 3 // 2, 128), bf16),
            vmem((2, 4, quarter, width), bf16),
            vmem((width, chip), bf16),
            vmem((16, width // 16, columns), bf16),
            vmem((2, 3, 4, width // 16, columns // 2), bf16),
            vmem((2, 4, width // 16, columns // 2), bf16),
            vmem((2, 3, width // 16, columns // 2), bf16),
            vmem((width // 16, columns), bf16),
            vmem((16, 8, 128), f32),
            vmem((4, 8, 128), f32),
            vmem((2, 8, 128), f32),
            vmem((3, 8, 128), f32),
            vmem((3, 4, 8, 128), f32),
            dma((3, 2, 4)), dma((3, 2, 3)), dma((3, 2, 3)), dma((2, 4)), dma((2, 3)), dma((2, 4)),
            dma((5, 2, 3)), dma((2, 2, 3)), dma((4, 2, 3)), dma((2,)),
        ],
        compiler_params=pltpu.CompilerParams(
            collective_id=2, has_side_effects=True, vmem_limit_bytes=60 << 20
        ),
    )(d_part, mix_part, middle, own_tokens, own_cot, gain_rows, weights, low, normed, qkv, attended, lse, start, table)


def halves(arrays):
    return jnp.stack(
        [
            jnp.concatenate([a[:, c * (a.shape[1] // 2) : (c + 1) * (a.shape[1] // 2)] for a in arrays], axis=1)
            for c in range(2)
        ]
    )


def angle_table(positions):
    half = HEAD_DIM // 2
    frequency = rope_base ** (-(jnp.arange(half, dtype=f32) * 2.0) / HEAD_DIM)
    angle = positions.astype(f32)[:, None] * frequency[None, :]
    cosine, sine = jnp.cos(angle), jnp.sin(angle)
    return jnp.concatenate([cosine, cosine, -sine, sine], axis=1)


def body(
    tokens_in,
    cotangent,
    segments,
    positions,
    norm1_gain,
    q_weight,
    k_weight,
    v_weight,
    o_weight,
    norm2_gain,
    gate_weight,
    up_weight,
    down_weight,
):
    rows, width = tokens_in.shape
    tensor, core = lax.axis_index("tensor"), lax.axis_index("core")
    quarter = rows // 4
    mlp_block = lax.all_to_all(halves((gate_weight, up_weight, down_weight.T)), "core", 0, 0)
    mlp_block = mlp_block.reshape(2 * gate_weight.shape[0], -1)
    mlp_full = lax.all_gather(mlp_block, ("shard", "x"), axis=0, tiled=True)
    gains = jnp.stack([norm1_gain, norm2_gain])
    gains = lax.dynamic_update_slice(jnp.zeros((16, 128), bf16), gains, (0, core * gains.shape[1]))
    seq_segs = segments[0]
    start = jnp.sum((seq_segs[:, None] < seq_segs[None, :]).astype(jnp.int32), axis=0)[None, :]
    full, _, chip_tokens, chip_cot, chip_table, normed_one, gain_rows = gather_attention(
        q_weight, k_weight, v_weight, o_weight.T, gains, tokens_in, cotangent, angle_table(positions)
    )
    weights = full.reshape(width, -1)
    table = chip_table.reshape(2 * rows, -1)
    qkv, low, attended, lse, middle, normed_two = attention_forward(
        normed_one, weights, table, start, chip_tokens, gain_rows
    )
    mixed, d_normed, terms = mlp(normed_two.reshape(2 * rows, width), chip_cot.reshape(2 * rows, width), mlp_full)
    mlp_grads = lax.psum_scatter(terms, ("shard", "x"), scatter_dimension=0, tiled=True)
    own_tokens = lax.dynamic_slice_in_dim(tokens_in, tensor * quarter, quarter)
    own_cot = lax.dynamic_slice_in_dim(cotangent, tensor * quarter, quarter)
    split = (2, 4, quarter, width)
    layer_out, input_grad, attn_grads, gain_grads = attention_backward(
        d_normed.reshape(split), mixed.reshape(split), middle, own_tokens, own_cot, gain_rows, weights,
        low, normed_one, qkv, attended, lse, start, table,
    )
    gain_own = lax.dynamic_slice(gain_grads, (0, core * norm1_gain.shape[0]), (2, norm1_gain.shape[0]))
    narrow = attn_grads.shape[2] // 4
    mlp_grads = mlp_grads.reshape(3, 2, rows // 4, -1).transpose(1, 0, 2, 3)
    mlp_grads = lax.all_to_all(mlp_grads, "core", 0, 0)

    def attn_of(k):
        piece = attn_grads[:, :, k * narrow : (k + 1) * narrow].astype(f32)
        return jnp.concatenate([piece[0], piece[1]], axis=1)

    def mlp_of(k):
        return jnp.concatenate([mlp_grads[0, k], mlp_grads[1, k]], axis=1).astype(f32)

    return (
        layer_out.reshape(rows, width),
        input_grad.reshape(rows, width),
        gain_own[0],
        attn_of(0),
        attn_of(1),
        attn_of(2),
        attn_of(3).T,
        gain_own[1],
        mlp_of(0),
        mlp_of(1),
        mlp_of(2).T,
    )


def solution(mesh):
    apart = Mesh(mesh.devices.reshape(4, 4, 2, 4), ("shard", "x", "core", "tensor"))
    tokens = ("shard", "x", "core")
    placed = (
        P(tokens, None),
        P(tokens, None),
        P("shard", None),
        P(tokens),
        P(tokens),
        P(tokens, "tensor"),
        P(tokens, "tensor"),
        P(tokens, "tensor"),
        P("tensor", tokens),
        P(tokens),
        P(tokens, "tensor"),
        P(tokens, "tensor"),
        P("tensor", tokens),
    )
    return jax.shard_map(
        body,
        mesh=apart,
        in_specs=placed,
        out_specs=(
            P(tokens, None),
            P(tokens, None),
            P(tokens),
            P(tokens, "tensor"),
            P(tokens, "tensor"),
            P(tokens, "tensor"),
            P("tensor", tokens),
            P(tokens),
            P(tokens, "tensor"),
            P(tokens, "tensor"),
            P("tensor", tokens),
        ),
        check_vma=False,
    )
```

time: 966 us -> 344 us (0.36); the launches traced: 951 us -> 342 us
  waiting for transfers between devices: 554 us -> 0.06 us
  Pallas kernels: 0 us -> 293 us
  local copies, waits for them, and re-layouts: 194 us -> 16.1 us
  matrix products: 151 us -> 0 us
  other arithmetic: 35.8 us -> 9.28 us
    pallas_call x0 -> x4, Pallas kernels: none -> 293 us  [the longest x1 126 us: attention_backward(): pl.pallas_call(backward_kernel, out_shape=(sds((4, quarter, width), bf16)...]
    unnamed x13 -> x3, waiting for transfers between devices: 205 us -> 0.03 us
    all_gather x3 -> x1, waiting for transfers between devices: 185 us -> 0.02 us  [body(): mlp_full = lax.all_gather(mlp_block, ('shard', 'x'), axis=0, tiled=True)]
    dot_general x49 -> x0, matrix products: 151 us -> none  [the longest x1 17 us: body(): jnp.einsum('tf,df->td', d_upper, up_full, preferred_element_type=jnp.floa...]
    psum x3 -> x0, waiting for transfers between devices: 127 us -> none  [the longest x1 45.2 us: body(): lax.psum((jnp.einsum('tf,df->td', d_gate, gate_full, preferred_element_ty...]
    concatenate x4 -> x0, local copies, waits for them, and re-layouts: 123 us -> none  [the longest x2 119 us: in_one_piece(): both = jnp.concatenate(columns, axis=along)]
    reduce_scatter x3 -> x0, waiting for transfers between devices: 36.6 us -> none  [the longest x1 30.1 us: in_one_piece_2(): lax.psum_scatter(both, axis, scatter_dimension=dim, tiled=True)]
    unnamed x64 -> x38, local copies, waits for them, and re-layouts: 43.9 us -> 9.24 us
  transfers between devices with their start and end apart: 11 -> 2, of which waited for: 10 -> 0; matrix products, arithmetic and copies ran while one was open for 22% -> 3% of each run, Pallas kernels for 0% -> 76%
where the time goes in v1:
time: 344 us; the launch traced here: 342 us
  Pallas kernels  293 us (85%)
  local copies, waits for them, and re-layouts  16.1 us (5%)
  between operations  14.4 us (4%)
  blocking collectives  9.63 us (3%)
  other arithmetic  9.28 us (3%)
    pallas_call x1, Pallas kernels, attention_backward(): pl.pallas_call(backward_kernel, out_shape=(sds((4, quarter, width), bf16)...  126 us
    pallas_call x1, Pallas kernels, attention_forward(): pl.pallas_call(forward_kernel, out_shape=(sds((3, seq, HEAD_DIM), bf16),...  80.1 us
    pallas_call x1, Pallas kernels, gather_attention(): pl.pallas_call(gather_kernel, out_shape=(sds((4, 4, 128, 2 * wq.shape[1])...  52.8 us
    pallas_call x1, Pallas kernels, mlp(): pl.pallas_call(mlp_kernel, grid=(steps,), out_shape=(sds((chip, width), b...  34.1 us
    unnamed x38, local copies, waits for them, and re-layouts  9.24 us
  transfers between devices with their start and end apart: 2, of which 0 were waited for; matrix products, arithmetic and copies ran while one was open for 3% of the time, Pallas kernels for 76%

profile of v1, /device:TPU:0, one launch (start us, length us, event | category | flops | bytes accessed | tf_op | source)
XLA Modules:
  0.0 342.3 jit_solution(8583823283608739261)
XLA Ops:
  7.2 0.0 copy-start.14
  7.2 0.0 copy-start.17
  7.2 0.0 copy-start.16
  7.2 0.0 copy-start.10
  7.3 0.0 all-gather.2.cloned.1.call-start
  7.3 1.1 fusion.1
  8.5 1.0 fusion.2
  9.4 1.0 fusion.3
  10.4 0.0 copy-start.15
  10.5 0.1 maximum_bitcast_fusion
  10.5 0.1 pad_maximum_fusion
  10.6 5.1 %all_to_all.10 = bf16[2,64,3072]{2,1,0:T(8,128)(2,1)} all-to-all(bf16[2,64,3072]{2,1,0:T(8,128)(2,1)S(1)} %pad_maximum_fusion), channel_id=1, replica_groups=mesh['shard'=4,'x'=4,'core'=2,'tensor'=4] {'core'}, dimensions={0} | all-to-all | bytes 1572864 | tf_op jit(solution)/shard_map/all_to_all | solution.py:741
  15.7 0.0 all-gather.2.cloned.1.call-update
  15.8 0.0 reduce-scatter.4.cloned.1.call-start
  15.9 0.3 dynamic_update_slice.3.gains
  16.2 0.5 multiply_cosine_fusion
  16.8 0.2 pad_maximum_fusion.1.table
  17.0 52.8 %shard_map.212 = (bf16[4,4,128,1024]{3,2,1,0:T(8,128)(2,1)S(1)}, bf16[4,4,2,16,128]{4,3,2,1,0:T(8,128)(2,1)}, bf16[2,256,2048]{2,1,0:T(8,128)(2,1)S(1)}, bf16[2,...) custom-call(bf16[64,512]{1,0:T(8,128)(2,1)S(1)} %copy-done.7, ...), custom_call_target="tpu_custom_call" | custom-call | tf_op jit(solution)/shard_map/pallas_call | solution.py:141
  69.8 2.0 copy-done
  71.8 1.3 copy-done.1
  73.1 1.3 copy-done.2
  74.4 0.7 copy-done.5
  75.1 0.6 copy-done.6
  75.8 1.3 copy-done.11
  77.1 2.3 convert_reduce_fusion
  79.4 80.1 %shard_map.213 = (bf16[3,2048,64]{2,1,0:T(8,128)(2,1)}, bf16[512,256]{1,0:T(8,128)(2,1)}, f32[2048,64]{1,0:T(8,128)}, f32[1,2048]{1,0:T(1,128)}, f32[64,2048]{1,0:T(8,128)}, /*index=5*/bf16[2,4,64,2048]{3,2,1,0:T(8,128)(2,1)}) custom-call(bf16[512,2048]{1,0:T(8,128)(2,1)} %copy-done.1, bf16[2048,1024]{1,0:T(8,128)(2,1)} %bitcast.60, f32[512,128]{1,0:T(8,128)} %bitcast.62, ...), custom_call_target="tpu_custom_call" | custom-call | tf_op jit(solution)/shard_map/pallas_call | solution.py:322
  159.5 0.0 all-gather.2.cloned.1.call-done.gate_w.up_w.down_w
  159.5 34.1 %shard_map.214 = (bf16[512,2048]{1,0:T(8,128)(2,1)}, bf16[512,2048]{1,0:T(8,128)(2,1)}, bf16[16,3,128,1024]{3,2,1,0:T(8,128)(2,1)}) custom-call(bf16[512,2048]{1,0:T(8,128)(2,1)} %bitcast.76, bf16[512,2048]{1,0:T(8,128)(2,1)} %bitcast.65, bf16[2048,3072]{1,0:T(8,128)(2,1)} %all-gather.2.cloned.1.call-done.gate_w.up_w.down_w, ...), custom_call_target="tpu_custom_call" | custom-call | flops 21474836480 | bytes 31457280 | tf_op jit(solution)/shard_map/pallas_call | solution.py:392
  193.5 0.0 reduce-scatter.4.cloned.1.call-update
  193.6 0.8 constant_dynamic-slice_fusion.1
  194.4 125.8 %shard_map.215 = (bf16[4,64,2048]{2,1,0:T(8,128)(2,1)}, bf16[4,64,2048]{2,1,0:T(8,128)(2,1)}, bf16[2,64,1024]{2,1,0:T(8,128)(2,1)}, f32[8,128]{1,0:T(8,128)}) custom-call(bf16[2,4,64,2048]{3,2,1,0:T(8,128)(2,1)} %bitcast.69, bf16[2,4,64,2048]{3,2,1,0:T(8,128)(2,1)} %bitcast.68, f32[64,2048]{1,0:T(8,128)} %get-tuple-element.39.middle, ...), custom_call_target="tpu_custom_call" | custom-call | tf_op jit(solution)/shard_map/pallas_call | solution.py:662
  320.2 0.8 constant_dynamic-slice_fusion
  321.0 1.0 slice_convert_fusion
  322.0 0.7 maximum_bitcast_fusion.2
  322.7 0.0 copy-start.13
  322.7 0.7 pad_maximum_fusion.4
  323.3 0.7 pad_maximum_fusion.3
  324.0 0.7 pad_maximum_fusion.2
  324.7 0.5 slice_bitcast_fusion.14
  325.2 1.2 copy.30
  326.4 0.0 copy-start.12
  326.4 4.5 %all_to_all.11 = bf16[2,3,64,1024]{3,2,1,0:T(8,128)(2,1)S(1)} all-to-all(bf16[2,3,64,1024]{3,2,1,0:T(8,128)(2,1)S(1)} %bitcast.67), channel_id=1, replica_groups=mesh['shard'=4,'x'=4,'core'=2,'tensor'=4] {'core'}, dimensions={0} | all-to-all | bytes 1572864 | tf_op jit(solution)/shard_map/all_to_all | solution.py:768
  330.9 0.1 slice_bitcast_fusion.1
  331.0 0.8 convert_bitcast_fusion
  331.8 0.8 maximum_convert_fusion.1
  332.7 0.8 maximum_convert_fusion
  333.5 1.0 copy.34
  334.5 1.0 copy.35
  (32 shorter events, 0.1 us)
Async XLA Ops:
  7.2 8.6 %copy-start.14 = (s32[256]{0:T(256)S(1)}, s32[256]{0:T(256)}, u32[]{:S(2)}) copy-start(s32[256]{0:T(256)} %param.16) | copy-start | bytes 3076
  7.2 8.6 %copy-start.17 = (bf16[64]{0:T(256)(128)(2,1)S(1)}, bf16[64]{0:T(256)(128)(2,1)}, u32[]{:S(2)}) copy-start(bf16[64]{0:T(256)(128)(2,1)} %param.17) | copy-start | bytes 388
  7.2 8.6 %copy-start.16 = (bf16[64]{0:T(256)(128)(2,1)S(1)}, bf16[64]{0:T(256)(128)(2,1)}, u32[]{:S(2)}) copy-start(bf16[64]{0:T(256)(128)(2,1)} %param.22) | copy-start | bytes 388
  7.2 9.7 %copy-start.10 = (bf16[512,64]{0,1:T(8,128)(2,1)S(1)}, bf16[512,64]{0,1:T(8,128)(2,1)}, u32[]{:S(2)}) copy-start(bf16[512,64]{0,1:T(8,128)(2,1)} %param.21) | copy-start | bytes 196612
  7.2 9.7 %copy-start.3 = (bf16[256,2048]{1,0:T(8,128)(2,1)S(1)}, bf16[256,2048]{1,0:T(8,128)(2,1)}, u32[]{:S(2)}) copy-start(bf16[256,2048]{1,0:T(8,128)(2,1)} %tokens.1) | copy-start | bytes 3145732
  7.2 9.7 %copy-start.4 = (bf16[256,2048]{1,0:T(8,128)(2,1)S(1)}, bf16[256,2048]{1,0:T(8,128)(2,1)}, u32[]{:S(2)}) copy-start(bf16[256,2048]{1,0:T(8,128)(2,1)} %cot.1) | copy-start | bytes 3145732
  7.2 9.7 %copy-start.7 = (bf16[64,512]{1,0:T(8,128)(2,1)S(1)}, bf16[64,512]{1,0:T(8,128)(2,1)}, u32[]{:S(2)}) copy-start(bf16[64,512]{1,0:T(8,128)(2,1)} %wq.1) | copy-start | bytes 196612
  7.3 9.7 %copy-start.8 = (bf16[64,512]{1,0:T(8,128)(2,1)S(1)}, bf16[64,512]{1,0:T(8,128)(2,1)}, u32[]{:S(2)}) copy-start(bf16[64,512]{1,0:T(8,128)(2,1)} %wk.1) | copy-start | bytes 196612
  7.3 9.7 %copy-start.9 = (bf16[64,512]{1,0:T(8,128)(2,1)S(1)}, bf16[64,512]{1,0:T(8,128)(2,1)}, u32[]{:S(2)}) copy-start(bf16[64,512]{1,0:T(8,128)(2,1)} %wv.1) | copy-start | bytes 196612
  7.3 152.2 %all-gather.2.cloned.1.call-start = ((), (), s32[]{:S(2)}) async-start(), calls=%async_computation.3 | async-start | bytes 13369344 | tf_op jit(solution)/shard_map/all_gather | solution.py:743
  10.4 66.6 %copy-start.15 = (s32[1,2048]{1,0:T(1,128)S(1)}, s32[1,2048]{1,0:T(1,128)}, u32[]{:S(2)}) copy-start(s32[1,2048]{1,0:T(1,128)} %param.15) | copy-start | bytes 24580
  15.8 309.5 %reduce-scatter.4.cloned.1.call-start = ((), (), s32[]{:S(2)}) async-start(), calls=%async_computation.4 | async-start | bytes 13369344
  69.8 2.0 copy-start
  71.8 1.3 copy-start.1
  73.1 1.3 copy-start.2
  74.4 0.7 copy-start.5
  75.1 0.6 copy-start.6
  75.8 1.3 copy-start.11
  322.7 10.8 %copy-start.13 = (bf16[4,64,2048]{2,1,0:T(8,128)(2,1)S(1)}, bf16[4,64,2048]{2,1,0:T(8,128)(2,1)}, u32[]{:S(2)}) copy-start(bf16[4,64,2048]{2,1,0:T(8,128)(2,1)} %get-tuple-element.44) | copy-start | bytes 3145732
  326.4 8.1 %copy-start.12 = (bf16[4,64,2048]{2,1,0:T(8,128)(2,1)S(1)}, bf16[4,64,2048]{2,1,0:T(8,128)(2,1)}, u32[]{:S(2)}) copy-start(bf16[4,64,2048]{2,1,0:T(8,128)(2,1)} %get-tuple-element.45) | copy-start | bytes 3145732
Sparse Core Ops, SparseCore 0:
  15.9 131.2 all-gather.1
  193.7 126.8 reduce-scatter.3
